TPU v7x, 32 devices: a whole 2x2x4 slice. The times are simulated.
32 devices in a mesh: sx: 8 (over y, x, core), sy: 4 (over z).
Axes of the slice: x: 2, y: 2, z: 4, core: 2. Of those that a mesh axis runs over, the one named last changes fastest.
Arguments:
- volume: bfloat16 [32, 128, 1024], P(None, 'sx', 'sy'), may hold values from -6 to 6
- w_first: bfloat16 [27, 32, 32], replicated, may hold values from -0.21875 to 0.21875
- down_weight: bfloat16 [2048, 128], replicated, may hold values from -0.125 to 0.125
- w_coarse: bfloat16 [4, 27, 128, 128], replicated, may hold values from -0.15625 to 0.15625
- w_up: bfloat16 [128, 2048], replicated, may hold values from -0.5 to 0.5
- closing_weight: bfloat16 [27, 32, 64], replicated, may hold values from -0.21875 to 0.21875
Outputs:
- result: bfloat16 [32, 128, 1024], P(None, 'sx', 'sy')
All inputs are finite; a program needn't handle non-finite values.
Results may differ from a plain program's by a relative error of at most 0.0095.
Values may be sent and summed in bfloat16 or wider, within the bound.
A program may use at most 64 MiB of HBM per device.

v0:
```python
import jax
import jax.numpy as jnp
from jax import lax
from jax.sharding import PartitionSpec as P

NZ = 16


def padded_2(array, sides, width):
    for axis, dim in sides:
        size, length = (lax.axis_size(axis), array.shape[dim])
        up = [(i, (i + 1) % size) for i in range(size - 1)]
        down = [(j, i) for i, j in up]
        last = lax.slice_in_dim(array, length - width, length, axis=dim)
        leading = lax.slice_in_dim(array, 0, width, axis=dim)
        before = lax.ppermute(last, axis, up)
        after = lax.ppermute(leading, axis, down)
        array = jnp.concatenate([before, array, after], axis=dim)
    return array


def fine_conv(padded, weight):
    in_width, broadened_x, flat = padded.shape
    voxel_count_x = broadened_x - 2
    voxel_count_y = flat // NZ - 2
    out_width = weight.shape[1]
    position = lax.broadcasted_iota(jnp.int32, (1, 1, flat), 2) % NZ
    bordered = jnp.pad(padded, ((0, 0), (0, 0), (1, 1)))
    shifted_list = []
    for offset_z in (-1, 0, 1):
        shifted = bordered[:, :, 1 + offset_z : 1 + offset_z + flat]
        inside = (position + offset_z >= 0) & (position + offset_z < NZ)
        shifted_list.append(jnp.where(inside, shifted, jnp.zeros_like(shifted)))
    stacked = jnp.concatenate(shifted_list, axis=0)
    kernel = (
        weight.reshape(3, 3, 3, out_width, in_width)
        .transpose(0, 1, 3, 2, 4)
        .reshape(9, out_width, 3 * in_width)
    )
    summed = jnp.zeros((out_width, voxel_count_x, voxel_count_y * NZ), jnp.float32)
    for offset in range(9):
        along_x = offset // 3
        along_y = offset % 3
        window = stacked[
            :, along_x : along_x + voxel_count_x, along_y * NZ : (along_y + voxel_count_y) * NZ
        ]
        summed = summed + jnp.einsum(
            "ok,kxf->oxf", kernel[offset], window, preferred_element_type=jnp.float32
        )
    return summed


def coarse_conv(padded, weight):
    span_x = padded.shape[0] - 2
    span_y = padded.shape[1] - 2
    span_z = padded.shape[2]
    in_width = padded.shape[3]
    out_width = weight.shape[1]
    extended = jnp.pad(padded, ((0, 0), (0, 0), (1, 1), (0, 0)))
    pieces = []
    for along_x in range(3):
        for along_y in range(3):
            for along_z in range(3):
                pieces.append(
                    extended[
                        along_x : along_x + span_x,
                        along_y : along_y + span_y,
                        along_z : along_z + span_z,
                        :,
                    ]
                )
    gathered = jnp.concatenate(pieces, axis=3).reshape(-1, 27 * in_width)
    kernel = weight.transpose(0, 2, 1).reshape(27 * in_width, out_width)
    summed = jnp.dot(gathered, kernel, preferred_element_type=jnp.float32)
    return jax.nn.relu(summed.reshape(span_x, span_y, span_z, out_width))


def strided_reduction(skip_features, down_weight, voxel_count_x, voxel_count_y):
    width = skip_features.shape[0]
    blocks = skip_features.reshape(
        width, voxel_count_x // 4, 4, voxel_count_y // 4, 4, NZ // 4, 4
    ).transpose(1, 3, 5, 0, 2, 4, 6)
    blocks = blocks.reshape(-1, width * 64)
    summed = jnp.dot(blocks, down_weight, preferred_element_type=jnp.float32)
    return summed.reshape(voxel_count_x // 4, voxel_count_y // 4, NZ // 4, down_weight.shape[1])


def expand(coarse_features, w_up):
    span_x, span_y, span_z, in_width = coarse_features.shape
    width = w_up.shape[1] // 64
    summed = jnp.dot(
        coarse_features.reshape(-1, in_width), w_up, preferred_element_type=jnp.float32
    ).astype(jnp.bfloat16)
    summed = summed.reshape(span_x, span_y, span_z, width, 4, 4, 4).transpose(3, 0, 4, 1, 5, 2, 6)
    return summed.reshape(width, 4 * span_x, 4 * span_y * NZ)


def local(volume, w_first, down_weight, w_coarse, w_up, closing_weight):
    width = volume.shape[0]
    voxel_count_x = volume.shape[1]
    voxel_count_y = volume.shape[2] // NZ
    padded = padded_2(
        volume.reshape(width, voxel_count_x, voxel_count_y, NZ), (("sx", 1), ("sy", 2)), 1
    )
    padded = padded.reshape(width, voxel_count_x + 2, (voxel_count_y + 2) * NZ)
    skip_features = jax.nn.relu(fine_conv(padded, w_first)).astype(jnp.bfloat16)
    coarse_features = strided_reduction(
        skip_features, down_weight, voxel_count_x, voxel_count_y
    ).astype(jnp.bfloat16)
    blocks_x = voxel_count_x // 4
    blocks_y = voxel_count_y // 4
    layers = w_coarse.shape[0]
    widened = padded_2(coarse_features, (("sx", 0), ("sy", 1)), layers)
    anchor_x = lax.axis_index("sx") * blocks_x
    anchor_y = lax.axis_index("sy") * blocks_y
    extent_x = blocks_x * lax.axis_size("sx")
    extent_y = blocks_y * lax.axis_size("sy")
    for layer_index in range(layers):
        margin = layers - layer_index - 1
        summed = coarse_conv(widened, w_coarse[layer_index])
        global_x = (
            lax.broadcasted_iota(jnp.int32, (summed.shape[0], 1, 1, 1), 0) + anchor_x - margin
        )
        global_y = (
            lax.broadcasted_iota(jnp.int32, (1, summed.shape[1], 1, 1), 1) + anchor_y - margin
        )
        keep = (global_x >= 0) & (global_x < extent_x) & (global_y >= 0) & (global_y < extent_y)
        widened = jnp.where(keep, summed, jnp.zeros_like(summed)).astype(jnp.bfloat16)
    coarse_features = widened
    upsampled = expand(coarse_features, w_up)
    joined = jnp.concatenate([skip_features, upsampled], axis=0)
    padded_last = padded_2(
        joined.reshape(2 * width, voxel_count_x, voxel_count_y, NZ), (("sx", 1), ("sy", 2)), 1
    )
    padded_last = padded_last.reshape(2 * width, voxel_count_x + 2, (voxel_count_y + 2) * NZ)
    return fine_conv(padded_last, closing_weight).astype(jnp.bfloat16)


def solution(mesh):
    return jax.shard_map(
        local,
        mesh=mesh,
        in_specs=(P(None, "sx", "sy"), P(), P(), P(), P(), P()),
        out_specs=P(None, "sx", "sy"),
        check_vma=False,
    )
```

profile of v0, /device:TPU:3, one launch (start us, length us, event | category | flops | bytes accessed | tf_op | source)
XLA Modules:
  0.0 151.5 jit_solution(16758181081597951425)
XLA Ops:
  0.0 1.5 %copy.21 = bf16[32,16,256]{0,2,1:T(8,128)(2,1)S(1)} copy(bf16[32,16,256]{2,1,0:T(8,128)(2,1)} %param.6) | data formatting | bytes 524288 | tf_op args[0]
  1.5 3.7 %collective-permute-start = (bf16[32,1,16,16]{0,3,2,1:T(8,128)(2,1)S(1)}, bf16[32,1,16,16]{0,3,2,1:T(8,128)(2,1)S(1)}, u32[]{:S(2)}, u32[]{:S(2)}) collective-permute-start(bf16[32,1,16,16]{0,3,2,1:T(8,128)(2,1)S(1)} %get-tuple-element.15), channel_id=1, source_target_pairs={{0,4},{4,8},{8,12},{12,16},{16,20},{20,24},{24,28},{1,5},{5,9},{9,... | collective-permute-start | bytes 49160 | tf_op jit(solution)/shard_map/ppermute | solution.py:16
  5.2 1.9 %collective-permute-start.1 = (bf16[32,1,16,16]{0,3,2,1:T(8,128)(2,1)S(1)}, bf16[32,1,16,16]{0,3,2,1:T(8,128)(2,1)S(1)}, u32[]{:S(2)}, u32[]{:S(2)}) collective-permute-start(bf16[32,1,16,16]{0,3,2,1:T(8,128)(2,1)S(1)} %get-tuple-element.16), channel_id=1, source_target_pairs={{4,0},{8,4},{12,8},{16,12},{20,16},{24,20},{28,24},{5,1},{9,5},{13... | collective-permute-start | bytes 49160 | tf_op jit(solution)/shard_map/ppermute | solution.py:17
  7.3 3.9 %slice_bitcast_fusion = (bf16[27,128,128]{1,2,0:T(8,128)(2,1)}, bf16[27,128,128]{1,2,0:T(8,128)(2,1)}, bf16[27,128,128]{1,2,0:T(8,128)(2,1)}, bf16[27,128,128]{1,2,0:T(8,128)(2,1)}) fusion(bf16[4,27,128,128]{3,2,1,0:T(8,128)(2,1)} %param.9), kind=kLoop, calls=%fused_computation.76 | loop fusion | bytes 7077888 | tf_op jit(solution)/shard_map/transpose | solution.py:73
  12.6 3.2 %collective-permute-start.2 = (bf16[32,18,1,16]{0,3,2,1:T(8,128)(2,1)S(1)}, bf16[32,18,1,16]{0,3,2,1:T(8,128)(2,1)S(1)}, u32[]{:S(2)}, u32[]{:S(2)}) collective-permute-start(bf16[32,18,1,16]{0,3,2,1:T(8,128)(2,1)S(1)} %get-tuple-element.13), channel_id=1, source_target_pairs={{0,1},{1,2},{2,3},{4,5},{5,6},{6,7},{8,9},{9,10},{10,11},{12,13},{... | collective-permute-start | bytes 55304 | tf_op jit(solution)/shard_map/ppermute | solution.py:16
  15.8 1.3 collective-permute-start.3
  17.5 3.4 %collective-permute-done.3 = bf16[32,18,1,16]{0,3,2,1:T(8,128)(2,1)S(1)} collective-permute-done((bf16[32,18,1,16]{0,3,2,1:T(8,128)(2,1)S(1)}, bf16[32,18,1,16]{0,3,2,1:T(8,128)(2,1)S(1)}, u32[]{:S(2)}, u32[]{:S(2)}) %collective-permute-start.3) | collective-permute-done | bytes 18464 | tf_op jit(solution)/shard_map/ppermute | solution.py:17
  26.5 11.3 %copy.27 = bf16[4,4,4,32,4,4,4]{6,5,4,3,2,1,0:T(4,128)(2,1)} copy(bf16[4,4,4,32,4,4,4]{3,6,2,5,1,4,0:T(4,128)(2,1)S(1)} %bitcast.146) | data formatting | bytes 524288 | tf_op jit(solution)/shard_map/transpose | solution.py:82
  37.7 17.3 %dot_general.103 = bf16[4,4,4,2048]{3,2,1,0:T(4,128)(2,1)} reshape(bf16[4,4,4,32,4,4,4]{6,5,4,3,2,1,0:T(4,128)(2,1)} %copy.27) | data formatting | bytes 524288 | tf_op jit(solution)/shard_map/dot_general | solution.py:84
  55.1 1.4 convolution_convert_fusion.1
  56.5 6.0 %collective-permute-start.4 = (bf16[4,4,4,128]{3,2,1,0:T(4,128)(2,1)S(1)}, bf16[4,4,4,128]{3,2,1,0:T(4,128)(2,1)S(1)}, u32[]{:S(2)}, u32[]{:S(2)}) collective-permute-start(bf16[4,4,4,128]{3,2,1,0:T(4,128)(2,1)S(1)} %convolution_convert_fusion.1), channel_id=1, source_target_pairs={{0,4},{4,8},{8,12},{12,16},{16,20},{20,24},{24,28},{1,5},{5,9},{9,... | collective-permute-start | bytes 49160 | tf_op jit(solution)/shard_map/ppermute | solution.py:16
  62.5 1.9 %collective-permute-start.5 = (bf16[4,4,4,128]{3,2,1,0:T(4,128)(2,1)S(1)}, bf16[4,4,4,128]{3,2,1,0:T(4,128)(2,1)S(1)}, u32[]{:S(2)}, u32[]{:S(2)}) collective-permute-start(bf16[4,4,4,128]{3,2,1,0:T(4,128)(2,1)S(1)} %convolution_convert_fusion.1), channel_id=1, source_target_pairs={{4,0},{8,4},{12,8},{16,12},{20,16},{24,20},{28,24},{5,1},{9,5},{13... | collective-permute-start | bytes 49160 | tf_op jit(solution)/shard_map/ppermute | solution.py:17
  64.4 4.0 %collective-permute-done.5 = bf16[4,4,4,128]{3,2,1,0:T(4,128)(2,1)S(1)} collective-permute-done((bf16[4,4,4,128]{3,2,1,0:T(4,128)(2,1)S(1)}, bf16[4,4,4,128]{3,2,1,0:T(4,128)(2,1)S(1)}, u32[]{:S(2)}, u32[]{:S(2)}) %collective-permute-start.5) | collective-permute-done | bytes 16416 | tf_op jit(solution)/shard_map/ppermute | solution.py:17
  68.5 3.2 %collective-permute-start.6 = (bf16[12,4,4,128]{3,2,1,0:T(4,128)(2,1)S(1)}, bf16[12,4,4,128]{3,2,1,0:T(4,128)(2,1)S(1)}, u32[]{:S(2)}, u32[]{:S(2)}) collective-permute-start(bf16[12,4,4,128]{3,2,1,0:T(4,128)(2,1)S(1)} %pad_maximum_fusion.14), channel_id=1, source_target_pairs={{0,1},{1,2},{2,3},{4,5},{5,6},{6,7},{8,9},{9,10},{10,11},{12,13},{... | collective-permute-start | bytes 147464 | tf_op jit(solution)/shard_map/ppermute | solution.py:16
  71.7 1.5 collective-permute-start.7
  73.2 1.3 and_and_fusion.3
  74.4 1.6 %copy.28 = bf16[27,128,128]{2,1,0:T(8,128)(2,1)} copy(bf16[27,128,128]{1,2,0:T(8,128)(2,1)S(1)} %copy-done.4) | data formatting | bytes 1769472 | tf_op jit(solution)/shard_map/transpose | solution.py:73
  76.1 1.7 %copy.30 = bf16[27,128,128]{2,1,0:T(8,128)(2,1)} copy(bf16[27,128,128]{1,2,0:T(8,128)(2,1)S(1)} %copy-done.3) | data formatting | bytes 1769472 | tf_op jit(solution)/shard_map/transpose | solution.py:73
  77.7 1.9 %copy.31 = bf16[27,128,128]{2,1,0:T(8,128)(2,1)S(1)} copy(bf16[27,128,128]{1,2,0:T(8,128)(2,1)} %get-tuple-element.8) | data formatting | bytes 1769472 | tf_op jit(solution)/shard_map/transpose | solution.py:73
  79.6 1.7 %copy.32 = bf16[27,128,128]{2,1,0:T(8,128)(2,1)} copy(bf16[27,128,128]{1,2,0:T(8,128)(2,1)S(1)} %copy-done.1) | data formatting | bytes 1769472 | tf_op jit(solution)/shard_map/transpose | solution.py:73
  84.1 1.3 fusion.59
  90.4 19.2 %reshape.404 = bf16[4,4,4,32,4,4,4]{6,5,4,3,2,1,0:T(4,128)(2,1)} reshape(bf16[64,2048]{1,0:T(8,128)(2,1)S(1)} %convolution_convert_fusion) | data formatting | bytes 524288 | tf_op jit(solution)/shard_map/reshape | solution.py:94
  109.6 12.8 %copy.34 = bf16[32,4,4,4,4,4,4]{0,6,5,4,3,2,1:T(4,128)(2,1)S(1)} copy(bf16[32,4,4,4,4,4,4]{6,4,2,0,5,3,1:T(4,128)(2,1)} %bitcast.145) | data formatting | bytes 524288 | tf_op jit(solution)/shard_map/transpose | solution.py:94
  122.5 2.2 %collective-permute-start.8 = (bf16[64,1,16,16]{0,3,2,1:T(8,128)(2,1)S(1)}, bf16[64,1,16,16]{0,3,2,1:T(8,128)(2,1)S(1)}, u32[]{:S(2)}, u32[]{:S(2)}) collective-permute-start(bf16[64,1,16,16]{0,3,2,1:T(8,128)(2,1)S(1)} %get-tuple-element.11), channel_id=1, source_target_pairs={{0,4},{4,8},{8,12},{12,16},{16,20},{20,24},{24,28},{1,5},{5,9},{9,... | collective-permute-start | bytes 98312 | tf_op jit(solution)/shard_map/ppermute | solution.py:16
  124.7 2.1 %collective-permute-start.9 = (bf16[64,1,16,16]{0,3,2,1:T(8,128)(2,1)S(1)}, bf16[64,1,16,16]{0,3,2,1:T(8,128)(2,1)S(1)}, u32[]{:S(2)}, u32[]{:S(2)}) collective-permute-start(bf16[64,1,16,16]{0,3,2,1:T(8,128)(2,1)S(1)} %get-tuple-element.12), channel_id=1, source_target_pairs={{4,0},{8,4},{12,8},{16,12},{20,16},{24,20},{28,24},{5,1},{9,5},{13... | collective-permute-start | bytes 98312 | tf_op jit(solution)/shard_map/ppermute | solution.py:17
  126.9 4.4 %collective-permute-done.9 = bf16[64,1,16,16]{0,3,2,1:T(8,128)(2,1)S(1)} collective-permute-done((bf16[64,1,16,16]{0,3,2,1:T(8,128)(2,1)S(1)}, bf16[64,1,16,16]{0,3,2,1:T(8,128)(2,1)S(1)}, u32[]{:S(2)}, u32[]{:S(2)}) %collective-permute-start.9) | collective-permute-done | bytes 32800 | tf_op jit(solution)/shard_map/ppermute | solution.py:17
  131.3 4.3 %collective-permute-start.10 = (bf16[64,18,1,16]{0,3,2,1:T(8,128)(2,1)S(1)}, bf16[64,18,1,16]{0,3,2,1:T(8,128)(2,1)S(1)}, u32[]{:S(2)}, u32[]{:S(2)}) collective-permute-start(bf16[64,18,1,16]{0,3,2,1:T(8,128)(2,1)S(1)} %get-tuple-element.9), channel_id=1, source_target_pairs={{0,1},{1,2},{2,3},{4,5},{5,6},{6,7},{8,9},{9,10},{10,11},{12,13},{... | collective-permute-start | bytes 110600 | tf_op jit(solution)/shard_map/ppermute | solution.py:16
  135.6 1.5 collective-permute-start.11
  137.5 3.2 %collective-permute-done.11 = bf16[64,18,1,16]{0,3,2,1:T(8,128)(2,1)S(1)} collective-permute-done((bf16[64,18,1,16]{0,3,2,1:T(8,128)(2,1)S(1)}, bf16[64,18,1,16]{0,3,2,1:T(8,128)(2,1)S(1)}, u32[]{:S(2)}, u32[]{:S(2)}) %collective-permute-start.11) | collective-permute-done | bytes 36896 | tf_op jit(solution)/shard_map/ppermute | solution.py:17
  140.7 1.7 %pad_maximum_fusion.3 = bf16[64,18,18,16]{0,3,2,1:T(8,128)(2,1)} fusion(bf16[64,18,1,16]{0,3,2,1:T(8,128)(2,1)S(1)} %collective-permute-done.11, bf16[64,1,16,16]{0,3,2,1:T(8,128)(2,1)S(1)} %collective-permute-done.9, bf16[32,16,16,16]{0,3,2,1:T(8,128)(2,1)S(1)} %bitcast.152, bf16[32,16,16,16]{0,3,2,1:T(8,128)(2,1)S(1)} %bitcast.149, ...), kind=kLoop, calls=%fused_computation.24 | loop fusion | flops 3981312 | bytes 1327104 | tf_op jit(solution)/shard_map/concatenate | solution.py:18
  142.4 1.8 %copy.35 = bf16[64,18,288]{2,0,1:T(8,128)(2,1)S(1)} copy(bf16[64,18,288]{0,2,1:T(8,128)(2,1)} %bitcast.156) | data formatting | bytes 1327104 | tf_op jit(solution)/shard_map/reshape | solution.py:135
  144.2 1.0 slice_select_fusion.1
  (195 shorter events, 21.5 us)
Async XLA Ops:
  0.0 90.2 %copy-start = (bf16[128,2048]{1,0:T(8,128)(2,1)S(1)}, bf16[128,2048]{1,0:T(8,128)(2,1)}, u32[]{:S(2)}) copy-start(bf16[128,2048]{1,0:T(8,128)(2,1)} %param.10) | copy-start | bytes 1572868
  1.5 11.0 %collective-permute-start = (bf16[32,1,16,16]{0,3,2,1:T(8,128)(2,1)S(1)}, bf16[32,1,16,16]{0,3,2,1:T(8,128)(2,1)S(1)}, u32[]{:S(2)}, u32[]{:S(2)}) collective-permute-start(bf16[32,1,16,16]{0,3,2,1:T(8,128)(2,1)S(1)} %get-tuple-element.15), channel_id=1, source_target_pairs={{0,4},{4,8},{8,12},{12,16},{16,20},{20,24},{24,28},{1,5},{5,9},{9,... | collective-permute-start | bytes 49160 | tf_op jit(solution)/shard_map/ppermute | solution.py:16
  5.2 7.3 %collective-permute-start.1 = (bf16[32,1,16,16]{0,3,2,1:T(8,128)(2,1)S(1)}, bf16[32,1,16,16]{0,3,2,1:T(8,128)(2,1)S(1)}, u32[]{:S(2)}, u32[]{:S(2)}) collective-permute-start(bf16[32,1,16,16]{0,3,2,1:T(8,128)(2,1)S(1)} %get-tuple-element.16), channel_id=1, source_target_pairs={{4,0},{8,4},{12,8},{16,12},{20,16},{24,20},{28,24},{5,1},{9,5},{13... | collective-permute-start | bytes 49160 | tf_op jit(solution)/shard_map/ppermute | solution.py:17
  7.3 9.9 %copy-start.7 = (bf16[27,32,32]{2,1,0:T(8,128)(2,1)S(1)}, bf16[27,32,32]{2,1,0:T(8,128)(2,1)}, u32[]{:S(2)}) copy-start(bf16[27,32,32]{2,1,0:T(8,128)(2,1)} %param.7) | copy-start | bytes 165892
  12.6 4.9 %collective-permute-start.2 = (bf16[32,18,1,16]{0,3,2,1:T(8,128)(2,1)S(1)}, bf16[32,18,1,16]{0,3,2,1:T(8,128)(2,1)S(1)}, u32[]{:S(2)}, u32[]{:S(2)}) collective-permute-start(bf16[32,18,1,16]{0,3,2,1:T(8,128)(2,1)S(1)} %get-tuple-element.13), channel_id=1, source_target_pairs={{0,1},{1,2},{2,3},{4,5},{5,6},{6,7},{8,9},{9,10},{10,11},{12,13},{... | collective-permute-start | bytes 55304 | tf_op jit(solution)/shard_map/ppermute | solution.py:16
  15.8 5.1 %collective-permute-start.3 = (bf16[32,18,1,16]{0,3,2,1:T(8,128)(2,1)S(1)}, bf16[32,18,1,16]{0,3,2,1:T(8,128)(2,1)S(1)}, u32[]{:S(2)}, u32[]{:S(2)}) collective-permute-start(bf16[32,18,1,16]{0,3,2,1:T(8,128)(2,1)S(1)} %get-tuple-element.14), channel_id=1, source_target_pairs={{1,0},{2,1},{3,2},{5,4},{6,5},{7,6},{9,8},{10,9},{11,10},{13,12},{... | collective-permute-start | bytes 55304 | tf_op jit(solution)/shard_map/ppermute | solution.py:17
  17.1 4.9 %copy-start.9 = (pred[288]{0:T(512)(128)(4,1)}, pred[288]{0:T(512)(128)(4,1)S(1)}, u32[]{:S(2)}) copy-start(pred[288]{0:T(512)(128)(4,1)S(1)} %compare_and_fusion.5) | copy-start | bytes 868
  37.7 36.7 %copy-start.4 = (bf16[27,128,128]{1,2,0:T(8,128)(2,1)S(1)}, bf16[27,128,128]{1,2,0:T(8,128)(2,1)}, u32[]{:S(2)}) copy-start(bf16[27,128,128]{1,2,0:T(8,128)(2,1)} %get-tuple-element.7) | copy-start | bytes 2654212
  55.1 21.0 %copy-start.3 = (bf16[27,128,128]{1,2,0:T(8,128)(2,1)S(1)}, bf16[27,128,128]{1,2,0:T(8,128)(2,1)}, u32[]{:S(2)}) copy-start(bf16[27,128,128]{1,2,0:T(8,128)(2,1)} %get-tuple-element.6) | copy-start | bytes 2654212
  56.5 7.9 %collective-permute-start.4 = (bf16[4,4,4,128]{3,2,1,0:T(4,128)(2,1)S(1)}, bf16[4,4,4,128]{3,2,1,0:T(4,128)(2,1)S(1)}, u32[]{:S(2)}, u32[]{:S(2)}) collective-permute-start(bf16[4,4,4,128]{3,2,1,0:T(4,128)(2,1)S(1)} %convolution_convert_fusion.1), channel_id=1, source_target_pairs={{0,4},{4,8},{8,12},{12,16},{16,20},{20,24},{24,28},{1,5},{5,9},{9,... | collective-permute-start | bytes 49160 | tf_op jit(solution)/shard_map/ppermute | solution.py:16
  62.5 6.0 %collective-permute-start.5 = (bf16[4,4,4,128]{3,2,1,0:T(4,128)(2,1)S(1)}, bf16[4,4,4,128]{3,2,1,0:T(4,128)(2,1)S(1)}, u32[]{:S(2)}, u32[]{:S(2)}) collective-permute-start(bf16[4,4,4,128]{3,2,1,0:T(4,128)(2,1)S(1)} %convolution_convert_fusion.1), channel_id=1, source_target_pairs={{4,0},{8,4},{12,8},{16,12},{20,16},{24,20},{28,24},{5,1},{9,5},{13... | collective-permute-start | bytes 49160 | tf_op jit(solution)/shard_map/ppermute | solution.py:17
  68.5 12.8 %collective-permute-start.6 = (bf16[12,4,4,128]{3,2,1,0:T(4,128)(2,1)S(1)}, bf16[12,4,4,128]{3,2,1,0:T(4,128)(2,1)S(1)}, u32[]{:S(2)}, u32[]{:S(2)}) collective-permute-start(bf16[12,4,4,128]{3,2,1,0:T(4,128)(2,1)S(1)} %pad_maximum_fusion.14), channel_id=1, source_target_pairs={{0,1},{1,2},{2,3},{4,5},{5,6},{6,7},{8,9},{9,10},{10,11},{12,13},{... | collective-permute-start | bytes 147464 | tf_op jit(solution)/shard_map/ppermute | solution.py:16
  71.7 9.6 %collective-permute-start.7 = (bf16[12,4,4,128]{3,2,1,0:T(4,128)(2,1)S(1)}, bf16[12,4,4,128]{3,2,1,0:T(4,128)(2,1)S(1)}, u32[]{:S(2)}, u32[]{:S(2)}) collective-permute-start(bf16[12,4,4,128]{3,2,1,0:T(4,128)(2,1)S(1)} %pad_maximum_fusion.14), channel_id=1, source_target_pairs={{1,0},{2,1},{3,2},{5,4},{6,5},{7,6},{9,8},{10,9},{11,10},{13,12},{... | collective-permute-start | bytes 147464 | tf_op jit(solution)/shard_map/ppermute | solution.py:17
  76.1 3.6 %copy-start.1 = (bf16[27,128,128]{1,2,0:T(8,128)(2,1)S(1)}, bf16[27,128,128]{1,2,0:T(8,128)(2,1)}, u32[]{:S(2)}) copy-start(bf16[27,128,128]{1,2,0:T(8,128)(2,1)} %get-tuple-element.5) | copy-start | bytes 2654212
  82.6 1.5 %copy-start.6 = (bf16[27,128,128]{2,1,0:T(8,128)(2,1)S(1)}, bf16[27,128,128]{2,1,0:T(8,128)(2,1)}, u32[]{:S(2)}) copy-start(bf16[27,128,128]{2,1,0:T(8,128)(2,1)} %copy.28) | copy-start | bytes 2654212
  82.6 1.5 %copy-start.12 = (pred[10,10]{1,0:T(8,128)(4,1)S(1)}, pred[10,10]{1,0:T(8,128)(4,1)}, u32[]{:S(2)}) copy-start(pred[10,10]{1,0:T(8,128)(4,1)} %and_and_fusion) | copy-start | bytes 304
  85.8 1.2 copy-start.2
  88.3 1.4 copy-start.5
  89.0 1.0 copy-start.11
  122.4 14.7 %copy-start.8 = (bf16[27,32,64]{2,1,0:T(8,128)(2,1)S(1)}, bf16[27,32,64]{2,1,0:T(8,128)(2,1)}, u32[]{:S(2)}) copy-start(bf16[27,32,64]{2,1,0:T(8,128)(2,1)} %param.11) | copy-start | bytes 331780
  122.5 4.3 %collective-permute-start.8 = (bf16[64,1,16,16]{0,3,2,1:T(8,128)(2,1)S(1)}, bf16[64,1,16,16]{0,3,2,1:T(8,128)(2,1)S(1)}, u32[]{:S(2)}, u32[]{:S(2)}) collective-permute-start(bf16[64,1,16,16]{0,3,2,1:T(8,128)(2,1)S(1)} %get-tuple-element.11), channel_id=1, source_target_pairs={{0,4},{4,8},{8,12},{12,16},{16,20},{20,24},{24,28},{1,5},{5,9},{9,... | collective-permute-start | bytes 98312 | tf_op jit(solution)/shard_map/ppermute | solution.py:16
  124.7 6.5 %collective-permute-start.9 = (bf16[64,1,16,16]{0,3,2,1:T(8,128)(2,1)S(1)}, bf16[64,1,16,16]{0,3,2,1:T(8,128)(2,1)S(1)}, u32[]{:S(2)}, u32[]{:S(2)}) collective-permute-start(bf16[64,1,16,16]{0,3,2,1:T(8,128)(2,1)S(1)} %get-tuple-element.12), channel_id=1, source_target_pairs={{4,0},{8,4},{12,8},{16,12},{20,16},{24,20},{28,24},{5,1},{9,5},{13... | collective-permute-start | bytes 98312 | tf_op jit(solution)/shard_map/ppermute | solution.py:17
  131.3 6.2 %collective-permute-start.10 = (bf16[64,18,1,16]{0,3,2,1:T(8,128)(2,1)S(1)}, bf16[64,18,1,16]{0,3,2,1:T(8,128)(2,1)S(1)}, u32[]{:S(2)}, u32[]{:S(2)}) collective-permute-start(bf16[64,18,1,16]{0,3,2,1:T(8,128)(2,1)S(1)} %get-tuple-element.9), channel_id=1, source_target_pairs={{0,1},{1,2},{2,3},{4,5},{5,6},{6,7},{8,9},{9,10},{10,11},{12,13},{... | collective-permute-start | bytes 110600 | tf_op jit(solution)/shard_map/ppermute | solution.py:16
  135.6 5.1 %collective-permute-start.11 = (bf16[64,18,1,16]{0,3,2,1:T(8,128)(2,1)S(1)}, bf16[64,18,1,16]{0,3,2,1:T(8,128)(2,1)S(1)}, u32[]{:S(2)}, u32[]{:S(2)}) collective-permute-start(bf16[64,18,1,16]{0,3,2,1:T(8,128)(2,1)S(1)} %get-tuple-element.10), channel_id=1, source_target_pairs={{1,0},{2,1},{3,2},{5,4},{6,5},{7,6},{9,8},{10,9},{11,10},{13,12},{... | collective-permute-start | bytes 110600 | tf_op jit(solution)/shard_map/ppermute | solution.py:17
  142.4 1.8 %copy-start.10 = (pred[288]{0:T(512)(128)(4,1)S(1)}, pred[288]{0:T(512)(128)(4,1)}, u32[]{:S(2)}) copy-start(pred[288]{0:T(512)(128)(4,1)} %copy-done.9) | copy-start | bytes 868
where the time goes:
time: 152 us
  local copies, waits for them, and re-layouts  82.7 us (54%)
  starting transfers between devices  32.8 us (22%)
  waiting for transfers between devices  15 us (10%)
  matrix products  12.9 us (8%)
  other arithmetic  7.25 us (5%)
    ppermute x6, starting transfers between devices, padded_2(): before = lax.ppermute(last, axis, up)  22.5 us
    reshape x1, local copies, waits for them, and re-layouts, expand(): summed.reshape(span_x, span_y, span_z, width, 4, 4, 4)  19.2 us
    dot_general x1, local copies, waits for them, and re-layouts, strided_reduction(): summed = jnp.dot(blocks, down_weight, preferred_element_type=jnp.float32)  17.3 us
    ppermute x6, waiting for transfers between devices, padded_2(): after = lax.ppermute(leading, axis, down)  15 us
    transpose x1, local copies, waits for them, and re-layouts, expand(): summed.reshape(span_x, span_y, span_z, width, 4, 4, 4)  12.8 us
    transpose x1, local copies, waits for them, and re-layouts, strided_reduction(): blocks = skip_features.reshape(width, voxel_count_x // 4, 4, voxel_count_...  11.3 us
    transpose x5, local copies, waits for them, and re-layouts, coarse_conv(): kernel = weight.transpose(0, 2, 1).reshape(27 * in_width, out_width)  10.8 us
    ppermute x6, starting transfers between devices, padded_2(): after = lax.ppermute(leading, axis, down)  10.2 us
  transfers between devices with their start and end apart: 12, of which 4 were waited for; matrix products, arithmetic and copies ran while one was open for 9% of the time, Pallas kernels for 0%

commit v1 on v0

v1 whole, which is shorter than its diff:
```python
import functools

import jax
import jax.numpy as jnp
from jax import lax
from jax.experimental import pallas as pl
from jax.experimental.pallas import tpu as pltpu
from jax.sharding import PartitionSpec as P

NZ = 16
S = 4
F32 = jnp.float32
BF = jnp.bfloat16
DIRS = [(dx, dy) for dx in (-1, 0, 1) for dy in (-1, 0, 1) if (dx, dy) != (0, 0)]
OPP = [DIRS.index((-dx, -dy)) for dx, dy in DIRS]
NT = (((1,), (1,)), ((), ()))
TN = (((0,), (0,)), ((), ()))


def dot(a, b, dims=(((1,), (0,)), ((), ()))):
    return lax.dot_general(a, b, dims, preferred_element_type=F32)


def banded(w, part, width):
    taps, out, inner = w.shape
    lanes = 2 * S * width
    shape = (inner, S * lanes)
    channel = lax.broadcasted_iota(jnp.int32, shape, 0)
    column = lax.broadcasted_iota(jnp.int32, shape, 1)
    zo = column // lanes
    lane = column % lanes
    quarter = lane // width
    zi = jnp.where(quarter < S, quarter, jnp.where(quarter == S, S, jnp.where(quarter == 2 * S - 1, -1, 99)))
    same = channel == lane % width + part * width
    w4 = w.reshape(taps // 3, 3, out, inner)
    total = None
    for tz in range(3):
        pick = jnp.where(same & (zi - zo + 1 == tz), 1.0, 0.0).astype(BF)
        term = dot(w4[:, tz].reshape(-1, inner), pick)
        total = term if total is None else total + term
    total = total.astype(BF).reshape(taps // 3, out, S * lanes)
    rows = [total[:, :, z * lanes : (z + 1) * lanes] for z in range(S)]
    return jnp.concatenate(rows, axis=1)


def spread(f_ref, a_ref, bx, rows, width, lo=0, hi=None):
    lanes = S * width
    hi = bx + 2 if hi is None else hi

    def step(x, carry):
        zb = lax.broadcasted_iota(jnp.int32, (rows, lanes), 0) % S
        lane = lax.broadcasted_iota(jnp.int32, (rows, lanes), 1)
        from_prev = (lane >= lanes - width) & (zb != 0)
        from_next = (lane < width) & (zb != S - 1)
        for dy in range(3):
            start = 4 + S * dy
            own = f_ref[x, start : start + rows, :]
            prev = f_ref[x, start - 1 : start - 1 + rows, :]
            after = f_ref[x, start + 1 : start + 1 + rows, :]
            edge = jnp.where(from_prev, prev, jnp.where(from_next, after, 0.0))
            a_ref[x, :, 2 * dy * lanes : (2 * dy + 1) * lanes] = own.astype(BF)
            a_ref[x, :, (2 * dy + 1) * lanes : (2 * dy + 2) * lanes] = edge.astype(BF)
        return carry

    lax.fori_loop(lo, hi, step, 0)


def fine(a_ref, b_ref, bx, rows):
    total = None
    for dx in range(3):
        a = a_ref[dx : dx + bx].reshape(bx * rows, a_ref.shape[2])
        term = dot(a, b_ref[dx], NT)
        total = term if total is None else total + term
    return total


def kernel(
    axes, x_ref, wf_ref, dw_ref, wc_hbm, up_ref, cw_ref, out_ref,
    f_ref, s_ref, a_ref, b1_ref, b2_ref, b3_ref, acc_ref, t_ref, c_ref, d_ref, wc_ref,
    send_f, recv_f, send_c, recv_c, wsem, ssem_f, rsem_f, ssem_c, rsem_c,
):
    ax, ay = axes
    nx, ny = lax.axis_size(ax), lax.axis_size(ay)
    ix, iy = lax.axis_index(ax), lax.axis_index(ay)
    bx, width, flat = x_ref.shape
    by = flat // NZ
    lanes = S * width
    rows = by * (NZ // S)
    ca, cb = bx // S, by // S
    cc = wc_ref.shape[2]
    layers = wc_ref.shape[0]
    crow = cb * S
    edge = bx * S

    weights = pltpu.make_async_copy(wc_hbm, wc_ref, wsem)
    weights.start()

    def exists(d):
        dx, dy = DIRS[d]
        ok = ix >= 0
        if dx:
            ok = ok & (ix + dx >= 0) & (ix + dx < nx)
        if dy:
            ok = ok & (iy + dy >= 0) & (iy + dy < ny)
        return ok

    def target(d):
        dx, dy = DIRS[d]
        return (ix + dx, iy + dy)

    barrier = pltpu.get_barrier_semaphore()
    for d in range(8):
        @pl.when(exists(d))
        def _(d=d):
            pl.semaphore_signal(barrier, inc=1, device_id=target(d), device_id_type=pl.DeviceIdType.MESH)

    def fine_copy(phase, d):
        count = 16 if DIRS[d][0] and DIRS[d][1] else (rows if DIRS[d][0] else edge)
        return pltpu.make_async_remote_copy(
            src_ref=send_f.at[phase, d, pl.ds(0, count)],
            dst_ref=recv_f.at[phase, OPP[d], pl.ds(0, count)],
            send_sem=ssem_f.at[phase, d],
            recv_sem=rsem_f.at[phase, OPP[d]],
            device_id=target(d),
            device_id_type=pl.DeviceIdType.MESH,
        )

    def coarse_copy(phase, d):
        return pltpu.make_async_remote_copy(
            src_ref=send_c.at[phase],
            dst_ref=recv_c.at[phase, OPP[d]],
            send_sem=ssem_c.at[phase, d],
            recv_sem=rsem_c.at[phase, OPP[d]],
            device_id=target(d),
            device_id_type=pl.DeviceIdType.MESH,
        )

    def each(make, act):
        for d in range(8):
            @pl.when(exists(d))
            def _(d=d):
                act(make(d), d)

    def start_all(make):
        each(make, lambda c, d: c.start())

    def sent_all(make):
        each(make, lambda c, d: c.wait_send())

    def recv_wait(copy_of):
        for d in range(8):
            @pl.when(exists(d))
            def _(d=d):
                copy_of(d).wait_recv()

    def fine_arrival(phase):
        def make(d):
            count = 16 if DIRS[d][0] and DIRS[d][1] else (rows if DIRS[d][0] else edge)
            return pltpu.make_async_remote_copy(
                src_ref=send_f.at[phase, d, pl.ds(0, count)],
                dst_ref=recv_f.at[phase, d, pl.ds(0, count)],
                send_sem=ssem_f.at[phase, d],
                recv_sem=rsem_f.at[phase, d],
                device_id=target(d),
                device_id_type=pl.DeviceIdType.MESH,
            )
        return make

    def coarse_arrival(phase):
        def make(d):
            return pltpu.make_async_remote_copy(
                src_ref=send_c.at[phase],
                dst_ref=recv_c.at[phase, d],
                send_sem=ssem_c.at[phase, d],
                recv_sem=rsem_c.at[phase, d],
                device_id=target(d),
                device_id_type=pl.DeviceIdType.MESH,
            )
        return make

    for d in range(8):
        @pl.when(jnp.logical_not(exists(d)))
        def _(d=d):
            recv_f[:, d] = jnp.zeros(recv_f.shape[:1] + recv_f.shape[2:], BF)
            recv_c[:, d] = jnp.zeros(recv_c.shape[:1] + recv_c.shape[2:], BF)

    def pack(ref, phase):
        t_ref[...] = jnp.zeros_like(t_ref)
        for d, (dx, dy) in enumerate(DIRS):
            x = 1 if dx < 0 else bx
            r = 8 if dy < 0 else 8 + rows - S
            if dx and dy:
                t_ref[d, 0:S] = ref[x, r : r + S]
            elif dy:
                for i in range(bx):
                    t_ref[d, S * i : S * (i + 1)] = ref[i + 1, r : r + S]
            if dx and not dy:
                send_f[phase, d, 0:rows] = ref[x, 8 : 8 + rows].astype(BF)
            else:
                send_f[phase, d] = t_ref[d].astype(BF)

    def unpack(ref, phase):
        for d, (dx, dy) in enumerate(DIRS):
            x = 0 if dx < 0 else bx + 1
            r = 4 if dy < 0 else 8 + rows
            if dx and not dy:
                ref[x, 8 : 8 + rows] = recv_f[phase, d, 0:rows].astype(F32)
            elif dx:
                ref[x, r : r + S] = recv_f[phase, d, 0:16].astype(F32)[0:S]
            else:
                t_ref[d, 0:edge] = recv_f[phase, d, 0:edge].astype(F32)
                for i in range(bx):
                    ref[i + 1, r : r + S] = t_ref[d, S * i : S * (i + 1)]

    group_r = lax.broadcasted_iota(jnp.int32, (rows, flat), 0)
    group_c = lax.broadcasted_iota(jnp.int32, (rows, flat), 1)
    select = jnp.where(group_c // S == group_r, 1.0, 0.0).astype(BF)
    quarter = lax.broadcasted_iota(jnp.int32, (lanes, flat), 0) // width
    in_quarter = (lax.broadcasted_iota(jnp.int32, (lanes, flat), 1) % S == quarter).astype(F32).astype(BF)
    for x in range(bx):
        one = x_ref[x]
        four = jnp.concatenate([one] * S, axis=0) * in_quarter
        f_ref[x + 1, 8 : 8 + rows] = dot(select, four, NT)

    pack(f_ref, 0)
    neighbours = sum(jnp.where(exists(d), 1, 0) for d in range(8))
    pl.semaphore_wait(barrier, neighbours)
    start_all(functools.partial(fine_copy, 0))

    def store_banded(ref, value):
        for k in range(9):
            ref[k // 3, :, (k % 3) * 2 * lanes : (k % 3 + 1) * 2 * lanes] = value[k]

    store_banded(b1_ref, banded(wf_ref[...], 0, width))
    store_banded(b2_ref, banded(cw_ref[...], 0, width))
    store_banded(b3_ref, banded(cw_ref[...], 1, width))

    recv_wait(fine_arrival(0))
    unpack(f_ref, 0)
    spread(f_ref, a_ref, bx, rows, width)
    skip = jnp.maximum(fine(a_ref, b1_ref, bx, rows), 0.0).astype(BF).astype(F32)
    s_ref[1 : bx + 1, 8 : 8 + rows] = skip.reshape(bx, rows, lanes)
    pack(s_ref, 1)
    start_all(functools.partial(fine_copy, 1))

    pieces = []
    for ox in range(S):
        for half in range(2):
            group = []
            for a in range(ca):
                for b in range(cb):
                    r = 8 + b * S * S + half * 2 * S
                    group.append(s_ref[1 + S * a + ox, r : r + 2 * S])
            pieces.append(jnp.concatenate(group, axis=0).astype(BF))
    lhs = jnp.concatenate(pieces, axis=1)
    down = []
    for parity in range(2):
        down.append(
            jnp.concatenate([dw_ref[S * ox + 2 * half + parity] for ox in range(S) for half in range(2)], axis=0)
        )
    both = [dot(lhs, w).reshape(ca * cb, 2 * S, cc) for w in down]
    t_down = both[0][:, 0:S] + both[1][:, S : 2 * S]
    for a in range(ca):
        for b in range(cb):
            d_ref[a, S * b : S * (b + 1)] = t_down[a * cb + b]
    send_c[0] = d_ref[...].reshape(ca * crow, cc).astype(BF)
    start_all(functools.partial(coarse_copy, 0))

    recv_wait(fine_arrival(1))
    unpack(s_ref, 1)
    spread(s_ref, a_ref, bx, rows, width)
    acc_ref[...] = fine(a_ref, b2_ref, bx, rows)

    weights.wait()
    recv_wait(coarse_arrival(0))

    def place(phase):
        for d, (dx, dy) in enumerate(DIRS):
            c_ref[ca * (dx + 1) : ca * (dx + 2), 8 + crow * (dy + 1) : 8 + crow * (dy + 2)] = (
                recv_c[phase, d].astype(F32).reshape(ca, crow, cc)
            )
        c_ref[ca : 2 * ca, 8 + crow : 8 + 2 * crow] = send_c[phase].astype(F32).reshape(ca, crow, cc)

    place(0)
    for layer in range(layers):
        margin = layers - 1 - layer
        na, nb = ca + 2 * margin, cb + 2 * margin
        n = nb * S
        off = layer
        zb = lax.broadcasted_iota(jnp.int32, (na, n, cc), 1) % S
        taps = []
        for da in range(3):
            for db in range(3):
                for dz in range(3):
                    r = 8 + S * (off + db) + dz - 1
                    v = c_ref[off + da : off + da + na, r : r + n]
                    if dz == 0:
                        v = jnp.where(zb != 0, v, 0.0)
                    if dz == 2:
                        v = jnp.where(zb != S - 1, v, 0.0)
                    taps.append(v.astype(BF).reshape(na * n, cc))
        lhs = jnp.concatenate(taps, axis=1)
        rhs = jnp.concatenate([wc_ref[layer, t] for t in range(27)], axis=1)
        summed = jnp.maximum(dot(lhs, rhs, NT), 0.0).reshape(na, n, cc)
        ga = lax.broadcasted_iota(jnp.int32, (na, n, cc), 0) + ix * ca - margin
        gb = lax.broadcasted_iota(jnp.int32, (na, n, cc), 1) // S + iy * cb - margin
        keep = (ga >= 0) & (ga < nx * ca) & (gb >= 0) & (gb < ny * cb)
        summed = jnp.where(keep, summed, 0.0).astype(BF).astype(F32)
        c_ref[off + 1 : off + 1 + na, 8 + S * (off + 1) : 8 + S * (off + 1) + n] = summed
    send_c[1] = c_ref[ca : 2 * ca, 8 + crow : 8 + 2 * crow].reshape(ca * crow, cc).astype(BF)
    start_all(functools.partial(coarse_copy, 1))
    recv_wait(coarse_arrival(1))
    place(1)

    cells = c_ref[ca - 1 : 2 * ca + 1, 8 + crow - S : 8 + 2 * crow + S]
    cells = cells.reshape((ca + 2) * (crow + 2 * S), cc).astype(BF)
    for ox in range(S):
        for oy in range(S):
            up = dot(cells, up_ref[S * ox + oy], NT).astype(BF).astype(F32)
            up = up.reshape(ca + 2, crow + 2 * S, lanes)
            for a in range(ca + 2):
                x = S * (a - 1) + ox + 1
                if x < 0 or x > bx + 1:
                    continue
                for b in range(cb + 2):
                    y = S * (b - 1) + oy
                    if y < -1 or y > by:
                        continue
                    f_ref[x, 8 + S * y : 8 + S * (y + 1)] = up[a, S * b : S * (b + 1)]

    spread(f_ref, a_ref, bx, rows, width)
    total = (acc_ref[...] + fine(a_ref, b3_ref, bx, rows)).astype(BF)
    for x in range(bx):
        one = dot(total[x * rows : (x + 1) * rows], select, TN)
        picked = jnp.where(in_quarter > 0, one, 0.0)
        res = picked[0:width]
        for z in range(1, S):
            res = res + picked[z * width : (z + 1) * width]
        out_ref[x] = res.astype(BF)

    for phase in range(2):
        sent_all(functools.partial(fine_copy, phase))
        sent_all(functools.partial(coarse_copy, phase))


def local(volume, w_first, down_weight, w_coarse, w_up, closing_weight):
    width, bx, flat = volume.shape
    by = flat // NZ
    lanes = S * width
    rows = by * (NZ // S)
    ca, crow = bx // S, by // S * S
    layers, _, cc, _ = w_coarse.shape
    cube = S * S * S
    down = down_weight.reshape(width, cube, cc).transpose(1, 0, 2).reshape(S * S, lanes, cc)
    up = w_up.T.reshape(width, cube, cc).transpose(1, 0, 2).reshape(S * S, lanes, cc)
    slot = max(rows, S * bx)
    vmem = pl.BlockSpec(memory_space=pltpu.VMEM)
    out = pl.pallas_call(
        functools.partial(kernel, ("sx", "sy")),
        out_shape=jax.ShapeDtypeStruct((bx, width, flat), BF),
        in_specs=[vmem, vmem, vmem, pl.BlockSpec(memory_space=pl.ANY), vmem, vmem],
        out_specs=vmem,
        scratch_shapes=[
            pltpu.VMEM((bx + 2, rows + 16, lanes), F32),
            pltpu.VMEM((bx + 2, rows + 16, lanes), F32),
            pltpu.VMEM((bx + 2, rows, 6 * lanes), BF),
            pltpu.VMEM((3, lanes, 6 * lanes), BF),
            pltpu.VMEM((3, lanes, 6 * lanes), BF),
            pltpu.VMEM((3, lanes, 6 * lanes), BF),
            pltpu.VMEM((bx * rows, lanes), F32),
            pltpu.VMEM((8, slot, lanes), F32),
            pltpu.VMEM((3 * ca, 3 * crow + 16, cc), F32),
            pltpu.VMEM((ca, crow, cc), F32),
            pltpu.VMEM(w_coarse.shape, BF),
            pltpu.VMEM((2, 8, slot, lanes), BF),
            pltpu.VMEM((2, 8, slot, lanes), BF),
            pltpu.VMEM((2, ca * crow, cc), BF),
            pltpu.VMEM((2, 8, ca * crow, cc), BF),
            pltpu.SemaphoreType.DMA,
            pltpu.SemaphoreType.DMA((2, 8)),
            pltpu.SemaphoreType.DMA((2, 8)),
            pltpu.SemaphoreType.DMA((2, 8)),
            pltpu.SemaphoreType.DMA((2, 8)),
        ],
        compiler_params=pltpu.CompilerParams(
            collective_id=0, has_side_effects=True, vmem_limit_bytes=48 * 1024 * 1024
        ),
    )(volume.transpose(1, 0, 2), w_first, down, w_coarse, up, closing_weight)
    return out.transpose(1, 0, 2)


def solution(mesh):
    return jax.shard_map(
        local,
        mesh=mesh,
        in_specs=(P(None, "sx", "sy"), P(), P(), P(), P(), P()),
        out_specs=P(None, "sx", "sy"),
        check_vma=False,
    )
```

time: 152 us -> 36.2 us (0.24)
  local copies, waits for them, and re-layouts: 82.7 us -> 8.71 us
  starting transfers between devices: 32.8 us -> 0 us
  Pallas kernels: 0 us -> 27.1 us
  waiting for transfers between devices: 15 us -> 0 us
  matrix products: 12.9 us -> 0 us
  other arithmetic: 7.25 us -> 0 us
    ppermute x12 -> x0, starting transfers between devices: 32.8 us -> none  [the longest x6 22.5 us: padded_2(): before = lax.ppermute(last, axis, up)]
    transpose x7 -> x2, local copies, waits for them, and re-layouts: 34.8 us -> 2.23 us  [the longest x1 1.38 us: local(): w_up.T.reshape(width, cube, cc).transpose(1, 0, 2).reshape(S * S, lanes, cc)]
    pallas_call x0 -> x1, Pallas kernels: none -> 27.1 us  [local(): pl.pallas_call(functools.partial(kernel, ('sx', 'sy')), out_shape=jax.Sha...]
    reshape x7 -> x1, local copies, waits for them, and re-layouts: 22.3 us -> 1.39 us  [local(): down_weight.reshape(width, cube, cc).transpose(1, 0, 2)]
    dot_general x1 -> x0, local copies, waits for them, and re-layouts: 17.3 us -> none  [strided_reduction(): summed = jnp.dot(blocks, down_weight, preferred_element_type=jnp.float32)]
    ppermute x12 -> x0, waiting for transfers between devices: 15 us -> none  [the longest x6 15 us: padded_2(): after = lax.ppermute(leading, axis, down)]
    dot_general x24 -> x0, matrix products: 12.9 us -> none  [the longest x18 8.33 us: fine_conv(): jnp.einsum('ok,kxf->oxf', kernel[offset], window, preferred_element_type=...]
    concatenate x6 -> x0, other arithmetic: 2.73 us -> none  [the longest x4 2.25 us: padded_2(): array = jnp.concatenate([before, array, after], axis=dim)]
  transfers between devices with their start and end apart: 12 -> 0, of which waited for: 4 -> 0; matrix products, arithmetic and copies ran while one was open for 9% -> 0% of each run, Pallas kernels for 0% -> 0%
where the time goes in v1:
time: 36.2 us; the launch traced here: 35.9 us
  Pallas kernels  27.1 us (75%)
  local copies, waits for them, and re-layouts  8.71 us (24%)
    pallas_call x1, Pallas kernels, local(): pl.pallas_call(functools.partial(kernel, ('sx', 'sy')), out_shape=jax.Sha...  27.1 us
    unnamed x8, local copies, waits for them, and re-layouts  5.09 us
    reshape x1, local copies, waits for them, and re-layouts, local(): down_weight.reshape(width, cube, cc).transpose(1, 0, 2)  1.39 us
    transpose x1, local copies, waits for them, and re-layouts, local(): w_up.T.reshape(width, cube, cc).transpose(1, 0, 2).reshape(S * S, lanes, cc)  1.38 us
    transpose x1, local copies, waits for them, and re-layouts, local(): return out.transpose(1, 0, 2)  0.85 us

profile of v1, /device:TPU:3, one launch (start us, length us, event | category | flops | bytes accessed | tf_op | source)
XLA Modules:
  0.0 35.9 jit_solution(10835963777812736521)
XLA Ops:
  0.0 0.0 copy-start
  0.0 2.2 %copy.13 = bf16[128,2048]{0,1:T(8,128)(2,1)} copy(bf16[128,2048]{1,0:T(8,128)(2,1)} %param.10) | data formatting | bytes 1048576 | tf_op args[4]
  2.2 1.4 %copy.14 = bf16[64,32,128]{2,1,0:T(8,128)(2,1)S(1)} copy(bf16[64,32,128]{2,0,1:T(8,128)(2,1)} %bitcast.18) | data formatting | bytes 1048576 | tf_op jit(solution)/shard_map/transpose | solution.py:355
  3.6 1.4 %copy.12 = bf16[32,64,128]{2,0,1:T(8,128)(2,1)S(1)} copy(bf16[32,64,128]{2,1,0:T(8,128)(2,1)} %bitcast.19) | data formatting | bytes 1048576 | tf_op jit(solution)/shard_map/reshape | solution.py:354
  5.0 1.0 %copy.17 = bf16[32,16,256]{2,0,1:T(8,128)(2,1)S(1)} copy(bf16[32,16,256]{2,1,0:T(8,128)(2,1)} %param.6) | data formatting | bytes 524288 | tf_op args[0]
  6.0 0.0 copy-done
  6.0 0.0 copy-start.1
  6.0 0.9 %copy-done.1 = bf16[27,32,32]{2,1,0:T(8,128)(2,1)S(1)} copy-done((bf16[27,32,32]{2,1,0:T(8,128)(2,1)S(1)}, bf16[27,32,32]{2,1,0:T(8,128)(2,1)}, u32[]{:S(2)}) %copy-start.1) | copy-done | bytes 55320
  7.0 0.0 copy-start.2
  7.0 0.9 %copy-done.2 = bf16[27,32,64]{2,1,0:T(8,128)(2,1)S(1)} copy-done((bf16[27,32,64]{2,1,0:T(8,128)(2,1)S(1)}, bf16[27,32,64]{2,1,0:T(8,128)(2,1)}, u32[]{:S(2)}) %copy-start.2) | copy-done | bytes 110616
  7.9 27.1 %shard_map.64 = bf16[16,32,256]{2,1,0:T(8,128)(2,1)S(1)} custom-call(bf16[16,32,256]{2,1,0:T(8,128)(2,1)S(1)} %bitcast.17, bf16[27,32,32]{2,1,0:T(8,128)(2,1)S(1)} %copy-done.1, bf16[16,128,128]{2,1,0:T(8,128)(2,1)S(1)} %bitcast.15, bf16[4,27,128,128]{3,2,1,0:T(8,128)(2,1)S(1)} %copy-done, bf16[16,128,128]{2,1,0:T(8,128)(2,1)S(1)} %bitcast.14, ...), custom_call_target="tpu_custom_call" | custom-call | tf_op jit(solution)/shard_map/pallas_call | solution.py:358
  35.0 0.9 %copy.15 = bf16[32,16,256]{2,1,0:T(8,128)(2,1)} copy(bf16[32,16,256]{2,0,1:T(8,128)(2,1)S(1)} %bitcast.16) | data formatting | bytes 524288 | tf_op jit(solution)/shard_map/transpose | solution.py:389
Async XLA Ops:
  0.0 6.0 %copy-start = (bf16[4,27,128,128]{3,2,1,0:T(8,128)(2,1)S(1)}, bf16[4,27,128,128]{3,2,1,0:T(8,128)(2,1)}, u32[]{:S(2)}) copy-start(bf16[4,27,128,128]{3,2,1,0:T(8,128)(2,1)} %wc_hbm.1) | copy-start | bytes 10616836
  6.0 0.9 %copy-start.1 = (bf16[27,32,32]{2,1,0:T(8,128)(2,1)S(1)}, bf16[27,32,32]{2,1,0:T(8,128)(2,1)}, u32[]{:S(2)}) copy-start(bf16[27,32,32]{2,1,0:T(8,128)(2,1)} %wf_ref.1) | copy-start | bytes 165892
  7.0 0.9 %copy-start.2 = (bf16[27,32,64]{2,1,0:T(8,128)(2,1)S(1)}, bf16[27,32,64]{2,1,0:T(8,128)(2,1)}, u32[]{:S(2)}) copy-start(bf16[27,32,64]{2,1,0:T(8,128)(2,1)} %cw_ref.1) | copy-start | bytes 331780

commit v2 on v1

--- a/solution.py
+++ b/solution.py
@@ -23,66 +23,66 @@
 
 def banded(w, part, width):
     taps, out, inner = w.shape
-    lanes = 2 * S * width
-    shape = (inner, S * lanes)
+    lanes = S * width
+    shape = (inner, 2 * S * lanes)
     channel = lax.broadcasted_iota(jnp.int32, shape, 0)
     column = lax.broadcasted_iota(jnp.int32, shape, 1)
-    zo = column // lanes
-    lane = column % lanes
-    quarter = lane // width
-    zi = jnp.where(quarter < S, quarter, jnp.where(quarter == S, S, jnp.where(quarter == 2 * S - 1, -1, 99)))
-    same = channel == lane % width + part * width
+    block = column // lanes
+    zi = column % lanes // width
+    zo = jnp.where(block < S, block, jnp.where(block == S, S, jnp.where(block == 2 * S - 1, -1, 99)))
+    same = channel == column % width + part * width
     w4 = w.reshape(taps // 3, 3, out, inner)
     total = None
     for tz in range(3):
         pick = jnp.where(same & (zi - zo + 1 == tz), 1.0, 0.0).astype(BF)
         term = dot(w4[:, tz].reshape(-1, inner), pick)
         total = term if total is None else total + term
-    total = total.astype(BF).reshape(taps // 3, out, S * lanes)
-    rows = [total[:, :, z * lanes : (z + 1) * lanes] for z in range(S)]
+    total = total.astype(BF).reshape(taps // 3, out, 2 * S * lanes)
+    rows = [total[:, :, z * lanes : (z + 1) * lanes] for z in range(2 * S)]
     return jnp.concatenate(rows, axis=1)
 
 
-def spread(f_ref, a_ref, bx, rows, width, lo=0, hi=None):
-    lanes = S * width
-    hi = bx + 2 if hi is None else hi
-
+def windows(v_ref, rows, *lead):
+    return [v_ref[(*lead, slice(4 + S * k, 4 + S * k + rows))].astype(BF) for k in range(3)]
+
+
+def spread(f_ref, a_ref, rows, lanes, lo, hi):
     def step(x, carry):
-        zb = lax.broadcasted_iota(jnp.int32, (rows, lanes), 0) % S
-        lane = lax.broadcasted_iota(jnp.int32, (rows, lanes), 1)
-        from_prev = (lane >= lanes - width) & (zb != 0)
-        from_next = (lane < width) & (zb != S - 1)
-        for dy in range(3):
-            start = 4 + S * dy
-            own = f_ref[x, start : start + rows, :]
-            prev = f_ref[x, start - 1 : start - 1 + rows, :]
-            after = f_ref[x, start + 1 : start + 1 + rows, :]
-            edge = jnp.where(from_prev, prev, jnp.where(from_next, after, 0.0))
-            a_ref[x, :, 2 * dy * lanes : (2 * dy + 1) * lanes] = own.astype(BF)
-            a_ref[x, :, (2 * dy + 1) * lanes : (2 * dy + 2) * lanes] = edge.astype(BF)
+        for k, v in enumerate(windows(f_ref, rows, x)):
+            a_ref[x, :, k * lanes : (k + 1) * lanes] = v
         return carry
 
     lax.fori_loop(lo, hi, step, 0)
 
 
 def fine(a_ref, b_ref, bx, rows):
-    total = None
-    for dx in range(3):
-        a = a_ref[dx : dx + bx].reshape(bx * rows, a_ref.shape[2])
-        term = dot(a, b_ref[dx], NT)
-        total = term if total is None else total + term
-    return total
+    a = jnp.concatenate([a_ref[k : k + bx].reshape(bx * rows, a_ref.shape[2]) for k in range(3)], axis=1)
+    b = jnp.concatenate([b_ref[k] for k in range(3)], axis=1)
+    return dot(a, b, NT)
+
+
+def joined_z(total, lanes, width):
+    n = total.shape[0]
+    own, other = total[:, :lanes], total[:, lanes:]
+    zb = lax.broadcasted_iota(jnp.int32, (n, lanes), 0) % S
+    lane = lax.broadcasted_iota(jnp.int32, (n, lanes), 1)
+    down = pltpu.roll(other, 1, 0)
+    up = pltpu.roll(other, n - 1, 0)
+    first = (lane < width) & (zb != 0)
+    last = (lane >= lanes - width) & (zb != S - 1)
+    return own + jnp.where(first, down, jnp.where(last, up, 0.0))
 
 
 def kernel(
-    axes, x_ref, wf_ref, dw_ref, wc_hbm, up_ref, cw_ref, out_ref,
-    f_ref, s_ref, a_ref, b1_ref, b2_ref, b3_ref, acc_ref, t_ref, c_ref, d_ref, wc_ref,
-    send_f, recv_f, send_c, recv_c, wsem, ssem_f, rsem_f, ssem_c, rsem_c,
+    axes, x_hbm, wf_hbm, dw_hbm, wc_hbm, up_hbm, cw_hbm, out_ref,
+    x_ref, wf_ref, dwo_ref, wc_ref, upo_ref, cw_ref,
+    v_ref, perm_ref, dw_ref, up_ref, f_ref, s_ref, a_ref, b1_ref, b2_ref, b3_ref, acc_ref, t_ref, h_ref,
+    c_ref, d_ref, o_ref, send_f, recv_f, send_c, recv_c, wsem, ssem_f, rsem_f, ssem_c, rsem_c,
 ):
     ax, ay = axes
     nx, ny = lax.axis_size(ax), lax.axis_size(ay)
     ix, iy = lax.axis_index(ax), lax.axis_index(ay)
-    bx, width, flat = x_ref.shape
+    width, bx, flat = x_ref.shape
     by = flat // NZ
     lanes = S * width
     rows = by * (NZ // S)
@@ -92,8 +92,10 @@
     crow = cb * S
     edge = bx * S
 
-    weights = pltpu.make_async_copy(wc_hbm, wc_ref, wsem)
-    weights.start()
+    pairs = [(x_hbm, x_ref), (wf_hbm, wf_ref), (cw_hbm, cw_ref), (dw_hbm, dwo_ref), (up_hbm, upo_ref), (wc_hbm, wc_ref)]
+    loads = [pltpu.make_async_copy(src, dst, wsem.at[k]) for k, (src, dst) in enumerate(pairs)]
+    for load in loads:
+        load.start()
 
     def exists(d):
         dx, dy = DIRS[d]
@@ -217,8 +219,13 @@
     select = jnp.where(group_c // S == group_r, 1.0, 0.0).astype(BF)
     quarter = lax.broadcasted_iota(jnp.int32, (lanes, flat), 0) // width
     in_quarter = (lax.broadcasted_iota(jnp.int32, (lanes, flat), 1) % S == quarter).astype(F32).astype(BF)
+    loads[0].wait()
+    hl = flat // 2
+    whole = x_ref[...].astype(F32).reshape(width * bx, flat)
+    for k in range(2):
+        v_ref[k] = whole[:, k * hl : (k + 1) * hl]
     for x in range(bx):
-        one = x_ref[x]
+        one = jnp.concatenate([v_ref[k, pl.ds(x, width, stride=bx), :] for k in range(2)], axis=1).astype(BF)
         four = jnp.concatenate([one] * S, axis=0) * in_quarter
         f_ref[x + 1, 8 : 8 + rows] = dot(select, four, NT)
 
@@ -229,16 +236,57 @@
 
     def store_banded(ref, value):
         for k in range(9):
-            ref[k // 3, :, (k % 3) * 2 * lanes : (k % 3 + 1) * 2 * lanes] = value[k]
-
+            ref[k // 3, :, (k % 3) * lanes : (k % 3 + 1) * lanes] = value[k]
+
+    def permuted(ref):
+        for k in range(S * S):
+            parts = [perm_ref[pl.ds(S * k + z, width, stride=S * S * S), :] for z in range(S)]
+            ref[k] = jnp.concatenate(parts, axis=0).astype(BF)
+
+    loads[1].wait()
     store_banded(b1_ref, banded(wf_ref[...], 0, width))
+    loads[2].wait()
     store_banded(b2_ref, banded(cw_ref[...], 0, width))
     store_banded(b3_ref, banded(cw_ref[...], 1, width))
+    loads[3].wait()
+    perm_ref[...] = dwo_ref[...].astype(F32)
+    permuted(dw_ref)
+    loads[4].wait()
+    for k in range(perm_ref.shape[0] // cc):
+        perm_ref[k * cc : (k + 1) * cc] = upo_ref[:, k * cc : (k + 1) * cc].astype(F32).T
+    permuted(up_ref)
+
+    def closing(ref, b_ref):
+        zero = jnp.zeros((S, lanes), F32)
+        for x in range(1, bx + 1):
+            ref[x, 8 - S : 8] = zero
+            ref[x, 8 + rows : 8 + rows + S] = zero
+        for x in (0, bx + 1):
+            a_ref[x] = jnp.zeros(a_ref.shape[1:], BF)
+        spread(ref, a_ref, rows, lanes, 1, bx + 1)
+        return fine(a_ref, b_ref, bx, rows).reshape(bx, rows, 2 * lanes)
+
+    def beside(phase, b_ref):
+        zero = jnp.zeros((S, lanes), F32)
+        for x, dx in ((0, -1), (bx - 1, 1)):
+            for k, dy in ((8 - S, -1), (8 + rows, 1)):
+                h_ref[k : k + S] = recv_f[phase, DIRS.index((dx, dy)), 0:16].astype(F32)[0:S]
+            h_ref[8 : 8 + rows] = recv_f[phase, DIRS.index((dx, 0)), 0:rows].astype(F32)
+            acc_ref[x] += dot(jnp.concatenate(windows(h_ref, rows), axis=1), b_ref[1 + dx], NT)
+        for r, dy in ((0, -1), (rows - S, 1)):
+            h_ref[8 - S : 8] = zero
+            h_ref[8 : 8 + edge] = recv_f[phase, DIRS.index((0, dy)), 0:edge].astype(F32)
+            h_ref[8 + edge : 8 + edge + S] = zero
+            b = jnp.concatenate([b_ref[k, :, (1 + dy) * lanes : (2 + dy) * lanes] for k in range(3)], axis=1)
+            part = dot(jnp.concatenate(windows(h_ref, edge), axis=1), b, NT)
+            for x in range(bx):
+                acc_ref[x, r : r + S] += part[S * x : S * (x + 1)]
 
     recv_wait(fine_arrival(0))
     unpack(f_ref, 0)
-    spread(f_ref, a_ref, bx, rows, width)
-    skip = jnp.maximum(fine(a_ref, b1_ref, bx, rows), 0.0).astype(BF).astype(F32)
+    spread(f_ref, a_ref, rows, lanes, 0, bx + 2)
+    skip = joined_z(fine(a_ref, b1_ref, bx, rows), lanes, width)
+    skip = jnp.maximum(skip, 0.0).astype(BF).astype(F32)
     s_ref[1 : bx + 1, 8 : 8 + rows] = skip.reshape(bx, rows, lanes)
     pack(s_ref, 1)
     start_all(functools.partial(fine_copy, 1))
@@ -266,12 +314,11 @@
     send_c[0] = d_ref[...].reshape(ca * crow, cc).astype(BF)
     start_all(functools.partial(coarse_copy, 0))
 
+    acc_ref[...] = closing(s_ref, b2_ref)
     recv_wait(fine_arrival(1))
-    unpack(s_ref, 1)
-    spread(s_ref, a_ref, bx, rows, width)
-    acc_ref[...] = fine(a_ref, b2_ref, bx, rows)
-
-    weights.wait()
+    beside(1, b2_ref)
+
+    loads[5].wait()
     recv_wait(coarse_arrival(0))
 
     def place(phase):
@@ -287,60 +334,57 @@
         na, nb = ca + 2 * margin, cb + 2 * margin
         n = nb * S
         off = layer
-        zb = lax.broadcasted_iota(jnp.int32, (na, n, cc), 1) % S
         taps = []
         for da in range(3):
             for db in range(3):
-                for dz in range(3):
-                    r = 8 + S * (off + db) + dz - 1
-                    v = c_ref[off + da : off + da + na, r : r + n]
-                    if dz == 0:
-                        v = jnp.where(zb != 0, v, 0.0)
-                    if dz == 2:
-                        v = jnp.where(zb != S - 1, v, 0.0)
-                    taps.append(v.astype(BF).reshape(na * n, cc))
+                r = 8 + S * (off + db)
+                taps.append(c_ref[off + da : off + da + na, r : r + n].astype(BF).reshape(na * n, cc))
         lhs = jnp.concatenate(taps, axis=1)
-        rhs = jnp.concatenate([wc_ref[layer, t] for t in range(27)], axis=1)
-        summed = jnp.maximum(dot(lhs, rhs, NT), 0.0).reshape(na, n, cc)
+        terms = []
+        for dz in range(3):
+            rhs = jnp.concatenate([wc_ref[layer, 3 * t + dz] for t in range(9)], axis=1)
+            terms.append(rhs)
+        product = dot(lhs, jnp.concatenate(terms, axis=0), NT)
+        zb = lax.broadcasted_iota(jnp.int32, (na * n, cc), 0) % S
+        summed = (
+            product[:, cc : 2 * cc]
+            + jnp.where(zb != 0, pltpu.roll(product[:, :cc], 1, 0), 0.0)
+            + jnp.where(zb != S - 1, pltpu.roll(product[:, 2 * cc :], na * n - 1, 0), 0.0)
+        )
+        summed = jnp.maximum(summed, 0.0).reshape(na, n, cc)
         ga = lax.broadcasted_iota(jnp.int32, (na, n, cc), 0) + ix * ca - margin
         gb = lax.broadcasted_iota(jnp.int32, (na, n, cc), 1) // S + iy * cb - margin
         keep = (ga >= 0) & (ga < nx * ca) & (gb >= 0) & (gb < ny * cb)
         summed = jnp.where(keep, summed, 0.0).astype(BF).astype(F32)
         c_ref[off + 1 : off + 1 + na, 8 + S * (off + 1) : 8 + S * (off + 1) + n] = summed
-    send_c[1] = c_ref[ca : 2 * ca, 8 + crow : 8 + 2 * crow].reshape(ca * crow, cc).astype(BF)
-    start_all(functools.partial(coarse_copy, 1))
-    recv_wait(coarse_arrival(1))
-    place(1)
-
-    cells = c_ref[ca - 1 : 2 * ca + 1, 8 + crow - S : 8 + 2 * crow + S]
-    cells = cells.reshape((ca + 2) * (crow + 2 * S), cc).astype(BF)
+    cells = c_ref[ca : 2 * ca, 8 + crow : 8 + 2 * crow].reshape(ca * crow, cc).astype(BF)
     for ox in range(S):
         for oy in range(S):
             up = dot(cells, up_ref[S * ox + oy], NT).astype(BF).astype(F32)
-            up = up.reshape(ca + 2, crow + 2 * S, lanes)
-            for a in range(ca + 2):
-                x = S * (a - 1) + ox + 1
-                if x < 0 or x > bx + 1:
-                    continue
-                for b in range(cb + 2):
-                    y = S * (b - 1) + oy
-                    if y < -1 or y > by:
-                        continue
-                    f_ref[x, 8 + S * y : 8 + S * (y + 1)] = up[a, S * b : S * (b + 1)]
-
-    spread(f_ref, a_ref, bx, rows, width)
-    total = (acc_ref[...] + fine(a_ref, b3_ref, bx, rows)).astype(BF)
+            for a in range(ca):
+                for b in range(cb):
+                    y = S * b + oy
+                    f_ref[S * a + ox + 1, 8 + S * y : 8 + S * (y + 1)] = up[a * crow + S * b : a * crow + S * (b + 1)]
+    pack(f_ref, 2)
+    start_all(functools.partial(fine_copy, 2))
+    acc_ref[...] += closing(f_ref, b3_ref)
+    recv_wait(fine_arrival(2))
+    beside(2, b3_ref)
+
+    total = joined_z(acc_ref[...].reshape(bx * rows, 2 * lanes), lanes, width).astype(BF)
     for x in range(bx):
         one = dot(total[x * rows : (x + 1) * rows], select, TN)
         picked = jnp.where(in_quarter > 0, one, 0.0)
         res = picked[0:width]
         for z in range(1, S):
             res = res + picked[z * width : (z + 1) * width]
-        out_ref[x] = res.astype(BF)
-
-    for phase in range(2):
+        for k in range(2):
+            o_ref[k, pl.ds(x, width, stride=bx), :] = res[:, k * hl : (k + 1) * hl]
+    out_ref[...] = jnp.concatenate([o_ref[0], o_ref[1]], axis=1).astype(BF).reshape(width, bx, flat)
+
+    for phase in range(3):
         sent_all(functools.partial(fine_copy, phase))
-        sent_all(functools.partial(coarse_copy, phase))
+    sent_all(functools.partial(coarse_copy, 0))
 
 
 def local(volume, w_first, down_weight, w_coarse, w_up, closing_weight):
@@ -350,43 +394,50 @@
     rows = by * (NZ // S)
     ca, crow = bx // S, by // S * S
     layers, _, cc, _ = w_coarse.shape
-    cube = S * S * S
-    down = down_weight.reshape(width, cube, cc).transpose(1, 0, 2).reshape(S * S, lanes, cc)
-    up = w_up.T.reshape(width, cube, cc).transpose(1, 0, 2).reshape(S * S, lanes, cc)
     slot = max(rows, S * bx)
     vmem = pl.BlockSpec(memory_space=pltpu.VMEM)
-    out = pl.pallas_call(
+    return pl.pallas_call(
         functools.partial(kernel, ("sx", "sy")),
-        out_shape=jax.ShapeDtypeStruct((bx, width, flat), BF),
-        in_specs=[vmem, vmem, vmem, pl.BlockSpec(memory_space=pl.ANY), vmem, vmem],
+        out_shape=jax.ShapeDtypeStruct((width, bx, flat), BF),
+        in_specs=[pl.BlockSpec(memory_space=pltpu.HBM)] * 6,
         out_specs=vmem,
         scratch_shapes=[
+            pltpu.VMEM(volume.shape, BF),
+            pltpu.VMEM(w_first.shape, BF),
+            pltpu.VMEM(down_weight.shape, BF),
+            pltpu.VMEM(w_coarse.shape, BF),
+            pltpu.VMEM(w_up.shape, BF),
+            pltpu.VMEM(closing_weight.shape, BF),
+            pltpu.VMEM((2, width * bx, flat // 2), F32),
+            pltpu.VMEM(down_weight.shape, F32),
+            pltpu.VMEM((S * S, lanes, cc), BF),
+            pltpu.VMEM((S * S, lanes, cc), BF),
             pltpu.VMEM((bx + 2, rows + 16, lanes), F32),
             pltpu.VMEM((bx + 2, rows + 16, lanes), F32),
-            pltpu.VMEM((bx + 2, rows, 6 * lanes), BF),
-            pltpu.VMEM((3, lanes, 6 * lanes), BF),
-            pltpu.VMEM((3, lanes, 6 * lanes), BF),
-            pltpu.VMEM((3, lanes, 6 * lanes), BF),
-            pltpu.VMEM((bx * rows, lanes), F32),
+            pltpu.VMEM((bx + 2, rows, 3 * lanes), BF),
+            pltpu.VMEM((3, 2 * lanes, 3 * lanes), BF),
+            pltpu.VMEM((3, 2 * lanes, 3 * lanes), BF),
+            pltpu.VMEM((3, 2 * lanes, 3 * lanes), BF),
+            pltpu.VMEM((bx, rows, 2 * lanes), F32),
             pltpu.VMEM((8, slot, lanes), F32),
+            pltpu.VMEM((slot + 16, lanes), F32),
             pltpu.VMEM((3 * ca, 3 * crow + 16, cc), F32),
             pltpu.VMEM((ca, crow, cc), F32),
-            pltpu.VMEM(w_coarse.shape, BF),
-            pltpu.VMEM((2, 8, slot, lanes), BF),
-            pltpu.VMEM((2, 8, slot, lanes), BF),
-            pltpu.VMEM((2, ca * crow, cc), BF),
-            pltpu.VMEM((2, 8, ca * crow, cc), BF),
-            pltpu.SemaphoreType.DMA,
-            pltpu.SemaphoreType.DMA((2, 8)),
-            pltpu.SemaphoreType.DMA((2, 8)),
-            pltpu.SemaphoreType.DMA((2, 8)),
-            pltpu.SemaphoreType.DMA((2, 8)),
+            pltpu.VMEM((2, width * bx, flat // 2), F32),
+            pltpu.VMEM((3, 8, slot, lanes), BF),
+            pltpu.VMEM((3, 8, slot, lanes), BF),
+            pltpu.VMEM((1, ca * crow, cc), BF),
+            pltpu.VMEM((1, 8, ca * crow, cc), BF),
+            pltpu.SemaphoreType.DMA((6,)),
+            pltpu.SemaphoreType.DMA((3, 8)),
+            pltpu.SemaphoreType.DMA((3, 8)),
+            pltpu.SemaphoreType.DMA((1, 8)),
+            pltpu.SemaphoreType.DMA((1, 8)),
         ],
         compiler_params=pltpu.CompilerParams(
-            collective_id=0, has_side_effects=True, vmem_limit_bytes=48 * 1024 * 1024
+            collective_id=0, has_side_effects=True, vmem_limit_bytes=62 * 1024 * 1024
         ),
-    )(volume.transpose(1, 0, 2), w_first, down, w_coarse, up, closing_weight)
-    return out.transpose(1, 0, 2)
+    )(volume, w_first, down_weight, w_coarse, w_up, closing_weight)
 
 
 def solution(mesh):

time: 36.2 us -> 23.4 us (0.65)
  local copies, waits for them, and re-layouts: 8.71 us -> 1.67 us
  Pallas kernels: 27.1 us -> 21.5 us
    pallas_call x1, Pallas kernels: 27.1 us -> 21.5 us  [local(): pl.pallas_call(functools.partial(kernel, ('sx', 'sy')), out_shape=jax.Sha...]
    unnamed x8 -> x1, local copies, waits for them, and re-layouts: 5.09 us -> 1.67 us
    transpose x2 -> x0, local copies, waits for them, and re-layouts: 2.23 us -> none  [the longest x1 1.38 us: local(): w_up.T.reshape(width, cube, cc).transpose(1, 0, 2).reshape(S * S, lanes, cc)]
    reshape x1 -> x0, local copies, waits for them, and re-layouts: 1.39 us -> none  [local(): down_weight.reshape(width, cube, cc).transpose(1, 0, 2)]
where the time goes in v2:
time: 23.4 us; the launch traced here: 23.2 us
  Pallas kernels  21.5 us (92%)
  local copies, waits for them, and re-layouts  1.67 us (7%)
    pallas_call x1, Pallas kernels, local(): pl.pallas_call(functools.partial(kernel, ('sx', 'sy')), out_shape=jax.Sha...  21.5 us
    unnamed x1, local copies, waits for them, and re-layouts  1.67 us

profile of v2, /device:TPU:3, one launch (start us, length us, event | category | flops | bytes accessed | tf_op | source)
XLA Modules:
  0.0 23.2 jit_solution(11794821951677797161)
XLA Ops:
  0.0 21.5 %shard_map.64 = bf16[32,16,256]{2,1,0:T(8,128)(2,1)} custom-call(bf16[32,16,256]{2,1,0:T(8,128)(2,1)} %x_hbm.1, bf16[27,32,32]{2,1,0:T(8,128)(2,1)} %wf_hbm.1, bf16[2048,128]{1,0:T(8,128)(2,1)} %dw_hbm.1, bf16[4,27,128,128]{3,2,1,0:T(8,128)(2,1)} %wc_hbm.1, bf16[128,2048]{1,0:T(8,128)(2,1)} %up_hbm.1, bf16[27,32,64]{2,1,0:T(8,128)(2,1)} %cw_hbm.1), custom_call_target="tpu_custom_call" | custom-call | tf_op jit(solution)/shard_map/pallas_call | solution.py:399
  21.6 1.7 %copy.8 = bf16[32,16,256]{2,1,0:T(8,128)(2,1)} copy(bf16[32,16,256]{2,1,0:T(8,128)(2,1)} %shard_map.64) | data formatting | bytes 524288

commit v3 on v2

--- a/solution.py
+++ b/solution.py
@@ -77,7 +77,7 @@
     axes, x_hbm, wf_hbm, dw_hbm, wc_hbm, up_hbm, cw_hbm, out_ref,
     x_ref, wf_ref, dwo_ref, wc_ref, upo_ref, cw_ref,
     v_ref, perm_ref, dw_ref, up_ref, f_ref, s_ref, a_ref, b1_ref, b2_ref, b3_ref, acc_ref, t_ref, h_ref,
-    c_ref, d_ref, o_ref, send_f, recv_f, send_c, recv_c, wsem, ssem_f, rsem_f, ssem_c, rsem_c,
+    c_ref, d_ref, send_f, recv_f, send_c, recv_c, wsem, ssem_f, rsem_f, ssem_c, rsem_c,
 ):
     ax, ay = axes
     nx, ny = lax.axis_size(ax), lax.axis_size(ay)
@@ -372,19 +372,30 @@
     beside(2, b3_ref)
 
     total = joined_z(acc_ref[...].reshape(bx * rows, 2 * lanes), lanes, width).astype(BF)
+    out_ref[...] = total
+
+    for phase in range(3):
+        sent_all(functools.partial(fine_copy, phase))
+    sent_all(functools.partial(coarse_copy, 0))
+
+
+def relayout(total_ref, out_ref, o_ref):
+    width, bx, flat = out_ref.shape
+    rows, lanes, hl = flat // S, S * width, flat // 2
+    group_r = lax.broadcasted_iota(jnp.int32, (rows, flat), 0)
+    group_c = lax.broadcasted_iota(jnp.int32, (rows, flat), 1)
+    select = jnp.where(group_c // S == group_r, 1.0, 0.0).astype(BF)
+    quarter = lax.broadcasted_iota(jnp.int32, (lanes, flat), 0) // width
+    in_quarter = lax.broadcasted_iota(jnp.int32, (lanes, flat), 1) % S == quarter
     for x in range(bx):
-        one = dot(total[x * rows : (x + 1) * rows], select, TN)
-        picked = jnp.where(in_quarter > 0, one, 0.0)
+        one = dot(total_ref[x * rows : (x + 1) * rows], select, TN)
+        picked = jnp.where(in_quarter, one, 0.0)
         res = picked[0:width]
         for z in range(1, S):
             res = res + picked[z * width : (z + 1) * width]
         for k in range(2):
             o_ref[k, pl.ds(x, width, stride=bx), :] = res[:, k * hl : (k + 1) * hl]
     out_ref[...] = jnp.concatenate([o_ref[0], o_ref[1]], axis=1).astype(BF).reshape(width, bx, flat)
-
-    for phase in range(3):
-        sent_all(functools.partial(fine_copy, phase))
-    sent_all(functools.partial(coarse_copy, 0))
 
 
 def local(volume, w_first, down_weight, w_coarse, w_up, closing_weight):
@@ -396,9 +407,9 @@
     layers, _, cc, _ = w_coarse.shape
     slot = max(rows, S * bx)
     vmem = pl.BlockSpec(memory_space=pltpu.VMEM)
-    return pl.pallas_call(
+    sums = pl.pallas_call(
         functools.partial(kernel, ("sx", "sy")),
-        out_shape=jax.ShapeDtypeStruct((width, bx, flat), BF),
+        out_shape=jax.ShapeDtypeStruct((bx * rows, lanes), BF),
         in_specs=[pl.BlockSpec(memory_space=pltpu.HBM)] * 6,
         out_specs=vmem,
         scratch_shapes=[
@@ -423,7 +434,6 @@
             pltpu.VMEM((slot + 16, lanes), F32),
             pltpu.VMEM((3 * ca, 3 * crow + 16, cc), F32),
             pltpu.VMEM((ca, crow, cc), F32),
-            pltpu.VMEM((2, width * bx, flat // 2), F32),
             pltpu.VMEM((3, 8, slot, lanes), BF),
             pltpu.VMEM((3, 8, slot, lanes), BF),
             pltpu.VMEM((1, ca * crow, cc), BF),
@@ -438,6 +448,14 @@
             collective_id=0, has_side_effects=True, vmem_limit_bytes=62 * 1024 * 1024
         ),
     )(volume, w_first, down_weight, w_coarse, w_up, closing_weight)
+    return pl.pallas_call(
+        relayout,
+        out_shape=jax.ShapeDtypeStruct((width, bx, flat), BF),
+        in_specs=[vmem],
+        out_specs=vmem,
+        scratch_shapes=[pltpu.VMEM((2, width * bx, flat // 2), F32)],
+        compiler_params=pltpu.CompilerParams(vmem_limit_bytes=16 * 1024 * 1024),
+    )(sums)
 
 
 def solution(mesh):

time: 23.4 us -> 23.1 us (0.987)
  local copies, waits for them, and re-layouts: 1.67 us -> 0.94 us
  Pallas kernels: 21.5 us -> 22 us
    pallas_call x0 -> x1, Pallas kernels: none -> 1.29 us  [local(): pl.pallas_call(relayout, out_shape=jax.ShapeDtypeStruct((width, bx, flat)...]
    pallas_call x1, Pallas kernels: 21.5 us -> 20.7 us  [local(): pl.pallas_call(functools.partial(kernel, ('sx', 'sy')), out_shape=jax.Sha...]
    unnamed x1 -> x2, local copies, waits for them, and re-layouts: 1.67 us -> 0.94 us
where the time goes in v3:
time: 23.1 us; the launch traced here: 23 us
  Pallas kernels  22 us (95%)
  local copies, waits for them, and re-layouts  0.94 us (4%)
    pallas_call x1, Pallas kernels, local(): pl.pallas_call(functools.partial(kernel, ('sx', 'sy')), out_shape=jax.Sha...  20.7 us
    pallas_call x1, Pallas kernels, local(): pl.pallas_call(relayout, out_shape=jax.ShapeDtypeStruct((width, bx, flat)...  1.29 us
    unnamed x2, local copies, waits for them, and re-layouts  0.94 us

profile of v3, /device:TPU:3, one launch (start us, length us, event | category | flops | bytes accessed | tf_op | source)
XLA Modules:
  0.0 23.0 jit_solution(12564084245016013442)
XLA Ops:
  0.0 20.7 %shard_map.64.total_ref = bf16[1024,128]{1,0:T(8,128)(2,1)} custom-call(bf16[32,16,256]{2,1,0:T(8,128)(2,1)} %x_hbm.1, bf16[27,32,32]{2,1,0:T(8,128)(2,1)} %wf_hbm.1, bf16[2048,128]{1,0:T(8,128)(2,1)} %dw_hbm.1, bf16[4,27,128,128]{3,2,1,0:T(8,128)(2,1)} %wc_hbm.1, bf16[128,2048]{1,0:T(8,128)(2,1)} %up_hbm.1, bf16[27,32,64]{2,1,0:T(8,128)(2,1)} %cw_hbm.1), custom_call_target="tpu_custom_call" | custom-call | tf_op jit(solution)/shard_map/pallas_call | solution.py:410
  20.8 0.0 copy-start
  20.8 0.9 %copy-done = bf16[1024,128]{1,0:T(8,128)(2,1)S(1)} copy-done((bf16[1024,128]{1,0:T(8,128)(2,1)S(1)}, bf16[1024,128]{1,0:T(8,128)(2,1)}, u32[]{:S(2)}) %copy-start) | copy-done | bytes 262168
  21.7 1.3 %shard_map.65 = bf16[32,16,256]{2,1,0:T(8,128)(2,1)} custom-call(bf16[1024,128]{1,0:T(8,128)(2,1)S(1)} %copy-done), custom_call_target="tpu_custom_call" | custom-call | tf_op jit(solution)/shard_map/pallas_call | solution.py:451
Async XLA Ops:
  20.8 1.0 %copy-start = (bf16[1024,128]{1,0:T(8,128)(2,1)S(1)}, bf16[1024,128]{1,0:T(8,128)(2,1)}, u32[]{:S(2)}) copy-start(bf16[1024,128]{1,0:T(8,128)(2,1)} %shard_map.64.total_ref) | copy-start | bytes 786436
